TPU v7x, 32 devices: a whole 2x2x4 slice. The times are simulated.
32 devices in a mesh: dp: 8 (over z, y), mp: 4 (over x, core).
Axes of the slice: x: 2, y: 2, z: 4, core: 2. Of those that a mesh axis runs over, the one named last changes fastest.
Arguments:
- chars: int32 [4096, 50], P('dp'), may hold values from 0 to 261
- char_mask: int32 [4096, 50], P('dp'), may hold values from 0 to 1, as said below
- word_order: int32 [4096], replicated, may hold values from 0 to 4095, as said below
- segment_ids: int32 [8, 512], P('dp'), may hold values from 0 to 7, never falling along the last dimension, each value on 1 to 128 neighbouring positions
- char_table: float32 [262, 16], replicated, may hold values from -6 to 6
- conv_weight: bfloat16 [112, 2048], P(None, 'mp'), may hold values from -0.75 to 0.75
- conv_bias: float32 [2048], P('mp'), may hold values from -3 to 3
- highway_weight: bfloat16 [2, 2048, 2, 2048], P(None, None, None, 'mp'), may hold values from -0.125 to 0.125
- highway_bias: float32 [2, 2, 2048], P(None, None, 'mp'), may hold values from -3 to 3
- project_weight: bfloat16 [2048, 768], P('mp'), may hold values from -0.125 to 0.125
- project_bias: float32 [768], replicated, may hold values from -3 to 3
- position_table: float32 [512, 768], replicated, may hold values from -5 to 5
- norm_gain: float32 [3, 768], replicated, may hold values from 0.5 to 1.5
- norm_bias: float32 [3, 768], replicated, may hold values from -2 to 2
- qkv_weight: bfloat16 [768, 3, 768], P(None, None, 'mp'), may hold values from -0.21875 to 0.21875
- qv_bias: float32 [2, 768], P(None, 'mp'), may hold values from -2 to 2
- out_weight: bfloat16 [768, 768], P('mp'), may hold values from -0.875 to 0.875
- out_bias: float32 [768], replicated, may hold values from -2 to 2
- up_weight: bfloat16 [768, 3072], P(None, 'mp'), may hold values from -0.21875 to 0.21875
- up_bias: float32 [3072], P('mp'), may hold values from -2 to 2
- down_weight: bfloat16 [3072, 768], P('mp'), may hold values from -0.109375 to 0.109375
- down_bias: float32 [768], replicated, may hold values from -2 to 2
- out_grad: float32 [4096, 768], P('dp'), may hold values from -6 to 6
Outputs:
- encoded: float32 [4096, 768], P('dp')
- char_table_grad: float32 [262, 16], replicated
- conv_weight_grad: float32 [112, 2048], P(None, 'mp')
- conv_bias_grad: float32 [2048], P('mp')
- highway_weight_grad: float32 [2, 2048, 2, 2048], P(None, 'dp', None, 'mp')
- highway_bias_grad: float32 [2, 2, 2048], P(None, None, 'mp')
- project_weight_grad: float32 [2048, 768], P('mp', 'dp')
- project_bias_grad: float32 [768], replicated
- position_table_grad: float32 [512, 768], replicated
- norm_gain_grad: float32 [3, 768], replicated
- norm_bias_grad: float32 [3, 768], replicated
- qkv_weight_grad: float32 [768, 3, 768], P('dp', None, 'mp')
- qv_bias_grad: float32 [2, 768], P(None, 'mp')
- out_weight_grad: float32 [768, 768], P('mp', 'dp')
- out_bias_grad: float32 [768], replicated
- up_weight_grad: float32 [768, 3072], P('dp', 'mp')
- up_bias_grad: float32 [3072], P('mp')
- down_weight_grad: float32 [3072, 768], P('mp', 'dp')
- down_bias_grad: float32 [768], replicated
Inputs may be any that keep to these rules, and one draw needn't show every extreme that they name: `char_mask`: each slot's mask is 1 on its first l characters and 0 after, 1 <= l <= 50; some slot has l = 50. `word_order`: a permutation of the tokens; cut the slots that one index s of dp holds into 8 equal runs in order, numbered d from 0; run d holds exactly the tokens of a share of the rows that index d of dp holds, every token of those rows in some run d of some index s; over the runs d of all indices s, taken in the order of s, words have at least as many characters in later runs.
All inputs are finite; a program needn't handle non-finite values.
Results may differ from a plain program's by a relative error of at most 0.023.
Values may be sent and summed in bfloat16 or wider, within the bound.
No kernel may reach another device: no remote copies, remote signals or barrier semaphores. Data moves between devices by JAX's collectives and lax.ppermute only.
A program may use at most 192 MiB of HBM per device.

v0:
```python
import jax
import jax.numpy as jnp
from jax import lax
from jax.sharding import PartitionSpec as P

HEAD = 64
CHANNELS = 2048
CHAR_DIM = 16
CHARS = 50
TAPS = 7
LAYERS = 2
ROW = 512


HIGH = lax.Precision.HIGHEST
EPSILON = 1e-05
NEGATIVE = -1e30


def filter_mask(local_count, first):
    channel = first + jnp.arange(local_count, dtype=jnp.int32)
    tap_count = 1 + sum(
        ((channel >= CHANNELS // divisor).astype(jnp.int32) for divisor in (64, 32, 16, 8, 4, 2))
    )
    tap_index = jnp.arange(TAPS * CHAR_DIM, dtype=jnp.int32) // CHAR_DIM
    return tap_index[:, None] < tap_count[None, :]


def char_windows(embedded):
    padded = jnp.pad(embedded, ((0, 0), (0, TAPS - 1), (0, 0)))
    return jnp.concatenate(
        [padded[:, offset : offset + CHARS, :] for offset in range(TAPS)], axis=2
    )


def layer_norm(values, gain_row, bias_row):
    center = values - jnp.mean(values, axis=-1, keepdims=True)
    spread = jnp.mean(center * center, axis=-1, keepdims=True)
    return center * lax.rsqrt(spread + EPSILON) * gain_row + bias_row


def embed_rows(ids_block, mask_block, char_table, filters, conv_bias):
    embedded = (
        jnp.take(char_table, ids_block, axis=0) * mask_block[..., None].astype(jnp.float32)
    ).astype(jnp.bfloat16)
    windows = char_windows(embedded)
    conv_out = (
        jnp.einsum("npk,kc->npc", windows, filters, preferred_element_type=jnp.float32) + conv_bias
    )
    return (windows, conv_out)


def pool_conv(conv_out):
    return jnp.mean(jax.nn.silu(conv_out), axis=1)


def block_size():
    return 128


def cnn_forward(ids_all, mask_all, char_table, filters, conv_bias):
    word_count = ids_all.shape[0]
    block_words = block_size()

    def one_block(block_pair):
        return pool_conv(
            embed_rows(block_pair[0], block_pair[1], char_table, filters, conv_bias)[1]
        )

    pooled = lax.map(
        one_block,
        (ids_all.reshape(-1, block_words, CHARS), mask_all.reshape(-1, block_words, CHARS)),
    )
    return pooled.reshape(word_count, -1)


def cnn_backward(ids_all, mask_all, pooled_grad, char_table, filters, conv_bias):
    block_words = block_size()
    vocab_ids = jnp.arange(char_table.shape[0], dtype=jnp.int32)

    def one_block(totals, pieces):
        ids_block, mask_block, grad_block = pieces
        windows, conv_out = embed_rows(ids_block, mask_block, char_table, filters, conv_bias)
        _, undo = jax.vjp(pool_conv, conv_out)
        conv_grad = undo(grad_block)[0].astype(jnp.bfloat16)
        weight_sum = totals[0] + jnp.einsum(
            "npk,npc->kc", windows, conv_grad, preferred_element_type=jnp.float32
        )
        bias_sum = totals[1] + jnp.sum(conv_grad.astype(jnp.float32), axis=(0, 1))
        window_grad = jnp.einsum(
            "npc,kc->npk", conv_grad, filters, preferred_element_type=jnp.float32
        )
        window_grad = window_grad.reshape(block_words, CHARS, TAPS, CHAR_DIM)
        padded = jnp.pad(window_grad, ((0, 0), (TAPS - 1, 0), (0, 0), (0, 0)))
        embed_grad = sum(
            (
                padded[:, TAPS - 1 - offset : TAPS - 1 - offset + CHARS, offset, :]
                for offset in range(TAPS)
            )
        )
        embed_grad = embed_grad * mask_block[..., None].astype(jnp.float32)
        onehot = (ids_block.reshape(-1)[:, None] == vocab_ids[None, :]).astype(jnp.float32)
        table_sum = totals[2] + jnp.einsum(
            "mv,me->ve", onehot, embed_grad.reshape(-1, CHAR_DIM), precision=HIGH
        )
        return ((weight_sum, bias_sum, table_sum), None)

    local_count = filters.shape[1]
    start_totals = (
        jnp.zeros(filters.shape, jnp.float32),
        jnp.zeros((local_count,), jnp.float32),
        jnp.zeros(char_table.shape, jnp.float32),
    )
    pieces = (
        ids_all.reshape(-1, block_words, CHARS),
        mask_all.reshape(-1, block_words, CHARS),
        pooled_grad.reshape(-1, block_words, local_count),
    )
    totals, _ = lax.scan(one_block, start_totals, pieces)
    return totals


def fold_rows(weights_now, piece):
    return jnp.einsum("nk,kjc->njc", piece, weights_now, preferred_element_type=jnp.float32)


def weight_rows(both_grad, piece):
    return jnp.einsum("nk,njc->kjc", piece, both_grad, preferred_element_type=jnp.float32)


def highway_mix(both_parts, carried):
    opened = jax.nn.sigmoid(both_parts[:, 1])
    return opened * jax.nn.silu(both_parts[:, 0]) + (1.0 - opened) * carried


def attend_scores(query_seq, key_seq, segment_row):
    scores = jnp.einsum(
        "qhe,khe->hqk", query_seq, key_seq, preferred_element_type=jnp.float32
    ) * HEAD ** (-0.5)
    same_doc = segment_row[:, None] == segment_row[None, :]
    return jnp.where(same_doc[None], scores, NEGATIVE)


def attend_forward(pieces):
    query_seq, key_seq, value_seq, segment_row = pieces
    scores = attend_scores(query_seq, key_seq, segment_row)
    row_max = jnp.max(scores, axis=-1, keepdims=True)
    total_lse = row_max + jnp.log(jnp.sum(jnp.exp(scores - row_max), axis=-1, keepdims=True))
    probs = jnp.exp(scores - total_lse).astype(jnp.bfloat16)
    mixed = jnp.einsum("hqk,khe->qhe", probs, value_seq, preferred_element_type=jnp.float32)
    return (mixed.astype(jnp.bfloat16), total_lse)


def attend_backward(pieces):
    query_seq, key_seq, value_seq, segment_row, lse_seq, grad_seq = pieces
    scores = attend_scores(query_seq, key_seq, segment_row)
    probs = jnp.exp(scores - lse_seq)
    prob_grad = jnp.einsum("qhe,khe->hqk", grad_seq, value_seq, preferred_element_type=jnp.float32)
    score_grad = (probs * (prob_grad - jnp.sum(probs * prob_grad, axis=-1, keepdims=True))).astype(
        jnp.bfloat16
    )
    scale_now = HEAD ** (-0.5)
    query_grad = (
        jnp.einsum("hqk,khe->qhe", score_grad, key_seq, preferred_element_type=jnp.float32)
        * scale_now
    )
    key_grad = (
        jnp.einsum("hqk,qhe->khe", score_grad, query_seq, preferred_element_type=jnp.float32)
        * scale_now
    )
    value_grad = jnp.einsum(
        "hqk,qhe->khe", probs.astype(jnp.bfloat16), grad_seq, preferred_element_type=jnp.float32
    )
    return (query_grad, key_grad, value_grad)


def column_sum(values):
    return jnp.sum(values.astype(jnp.float32), axis=0)


def on_device(
    chars,
    char_mask,
    word_order,
    segment_ids,
    char_table,
    conv_weight,
    conv_bias,
    highway_weight,
    highway_bias,
    project_weight,
    project_bias,
    position_table,
    norm_gain,
    norm_bias,
    qkv_weight,
    qv_bias,
    out_weight,
    out_bias,
    up_weight,
    up_bias,
    down_weight,
    down_bias,
    out_grad,
):
    dp_count = lax.axis_size("dp")
    dp_index = lax.axis_index("dp")
    word_count = chars.shape[0]
    seq_count = word_count // ROW
    per_peer = word_count // dp_count
    local_rows = (
        lax.dynamic_slice(
            word_order.reshape(dp_count, dp_count, per_peer),
            (0, dp_index, 0),
            (dp_count, 1, per_peer),
        ).reshape(word_count)
        - dp_index * word_count
    )
    ordering = (
        jnp.zeros((word_count,), jnp.int32)
        .at[local_rows]
        .set(jnp.arange(word_count, dtype=jnp.int32))
    )
    local_channels = conv_weight.shape[1]
    used_taps = filter_mask(local_channels, lax.axis_index("mp") * local_channels)
    filters = jnp.where(used_taps, conv_weight, jnp.zeros_like(conv_weight))
    pooled = cnn_forward(chars, char_mask, char_table, filters, conv_bias).astype(jnp.bfloat16)
    first_state = lax.all_to_all(pooled, "dp", split_axis=0, concat_axis=0, tiled=True)[ordering]
    carried = first_state.astype(jnp.float32)
    inputs = first_state
    kept = []
    for depth_index in range(LAYERS):
        weights_now = highway_weight[depth_index]
        both_parts = (
            fold_rows(weights_now, lax.all_gather(inputs, "mp", axis=1, tiled=True))
            + highway_bias[depth_index]
        )
        kept.append((inputs, carried, both_parts))
        carried = highway_mix(both_parts, carried)
        inputs = carried.astype(jnp.bfloat16)
    embed_sum = (
        lax.psum(jnp.dot(inputs, project_weight, preferred_element_type=jnp.float32), "mp")
        + project_bias
    )
    embed_total = (embed_sum.reshape(seq_count, ROW, -1) + position_table).reshape(word_count, -1)
    hidden_in = layer_norm(embed_total, norm_gain[0], norm_bias[0])
    x_low = hidden_in.astype(jnp.bfloat16)
    qkv_out = jnp.einsum("nd,djh->njh", x_low, qkv_weight, preferred_element_type=jnp.float32)
    query = (qkv_out[:, 0] + qv_bias[0]).astype(jnp.bfloat16)
    keys_all = qkv_out[:, 1].astype(jnp.bfloat16)
    values_all = (qkv_out[:, 2] + qv_bias[1]).astype(jnp.bfloat16)
    head_shape = (seq_count, ROW, qkv_weight.shape[2] // HEAD, HEAD)
    attn_in = (
        query.reshape(head_shape),
        keys_all.reshape(head_shape),
        values_all.reshape(head_shape),
        segment_ids,
    )
    mixed, lse_all = lax.map(attend_forward, attn_in)
    mixed = mixed.reshape(word_count, -1)
    attended = (
        lax.psum(jnp.dot(mixed, out_weight, preferred_element_type=jnp.float32), "mp") + out_bias
    )
    resid_one = hidden_in + attended
    hidden_mid = layer_norm(resid_one, norm_gain[1], norm_bias[1])
    mid_low = hidden_mid.astype(jnp.bfloat16)
    upward = jnp.dot(mid_low, up_weight, preferred_element_type=jnp.float32) + up_bias
    activated = jax.nn.gelu(upward).astype(jnp.bfloat16)
    downward = (
        lax.psum(jnp.dot(activated, down_weight, preferred_element_type=jnp.float32), "mp")
        + down_bias
    )
    resid_two = hidden_mid + downward
    encoded = layer_norm(resid_two, norm_gain[2], norm_bias[2])
    _, undo = jax.vjp(layer_norm, resid_two, norm_gain[2], norm_bias[2])
    resid_two_grad, gain_two, shift_two = undo(out_grad)
    down_grad = resid_two_grad.astype(jnp.bfloat16)
    down_bias_grad = column_sum(down_grad)
    down_weight_grad = jnp.einsum(
        "nf,nd->fd", activated, down_grad, preferred_element_type=jnp.float32
    )
    act_grad = jnp.einsum("nd,fd->nf", down_grad, down_weight, preferred_element_type=jnp.float32)
    _, undo = jax.vjp(jax.nn.gelu, upward)
    up_grad = undo(act_grad)[0].astype(jnp.bfloat16)
    up_bias_grad = column_sum(up_grad)
    up_weight_grad = jnp.einsum("nd,nf->df", mid_low, up_grad, preferred_element_type=jnp.float32)
    mid_part = jnp.einsum("nf,df->nd", up_grad, up_weight, preferred_element_type=jnp.float32)
    mid_grad = resid_two_grad + lax.psum(mid_part, "mp")
    _, undo = jax.vjp(layer_norm, resid_one, norm_gain[1], norm_bias[1])
    resid_one_grad, gain_one, shift_one = undo(mid_grad)
    attn_grad = resid_one_grad.astype(jnp.bfloat16)
    out_bias_grad = column_sum(attn_grad)
    out_weight_grad = jnp.einsum("nh,nd->hd", mixed, attn_grad, preferred_element_type=jnp.float32)
    mixed_grad = jnp.einsum(
        "nd,hd->nh", attn_grad, out_weight, preferred_element_type=jnp.float32
    ).astype(jnp.bfloat16)
    query_grad, key_grad, value_grad = lax.map(
        attend_backward, attn_in + (lse_all, mixed_grad.reshape(head_shape))
    )
    qkv_grad = jnp.stack(
        [
            query_grad.reshape(word_count, -1).astype(jnp.bfloat16),
            key_grad.reshape(word_count, -1).astype(jnp.bfloat16),
            value_grad.reshape(word_count, -1).astype(jnp.bfloat16),
        ],
        axis=1,
    )
    qv_bias_grad = jnp.stack([column_sum(qkv_grad[:, 0]), column_sum(qkv_grad[:, 2])], axis=0)
    qkv_weight_grad = jnp.einsum("nd,njh->djh", x_low, qkv_grad, preferred_element_type=jnp.float32)
    x_part = jnp.einsum("njh,djh->nd", qkv_grad, qkv_weight, preferred_element_type=jnp.float32)
    hidden_grad = resid_one_grad + lax.psum(x_part.astype(jnp.bfloat16), "mp").astype(jnp.float32)
    _, undo = jax.vjp(layer_norm, embed_total, norm_gain[0], norm_bias[0])
    embed_grad, gain_zero, shift_zero = undo(hidden_grad)
    position_grad = jnp.sum(embed_grad.reshape(seq_count, ROW, -1), axis=0)
    proj_grad = embed_grad.astype(jnp.bfloat16)
    project_bias_grad = column_sum(proj_grad)
    project_weight_grad = jnp.einsum(
        "nc,nd->cd", inputs, proj_grad, preferred_element_type=jnp.float32
    )
    state_grad = jnp.einsum(
        "nd,cd->nc", proj_grad, project_weight, preferred_element_type=jnp.float32
    )
    level_weight_grads = [None] * LAYERS
    level_bias_grads = [None] * LAYERS
    for depth_index in reversed(range(LAYERS)):
        inputs_now, carried_now, both_now = kept[depth_index]
        _, undo = jax.vjp(highway_mix, both_now, carried_now)
        both_grad, carried_grad = undo(state_grad)
        both_grad = both_grad.astype(jnp.bfloat16)
        level_bias_grads[depth_index] = column_sum(both_grad)
        level_weight_grads[depth_index] = weight_rows(
            both_grad, lax.all_gather(inputs_now, "mp", axis=1, tiled=True)
        )
        input_part = jnp.einsum(
            "njc,kjc->nk",
            both_grad,
            highway_weight[depth_index],
            preferred_element_type=jnp.float32,
        )
        state_grad = (
            lax.psum_scatter(
                input_part.astype(jnp.bfloat16), "mp", scatter_dimension=1, tiled=True
            ).astype(jnp.float32)
            + carried_grad
        )
    highway_weight_grad = jnp.stack(level_weight_grads, axis=0)
    highway_bias_grad = jnp.stack(level_bias_grads, axis=0)
    pooled_grad = state_grad.astype(jnp.bfloat16)
    cnn_grad = lax.all_to_all(
        pooled_grad[local_rows], "dp", split_axis=0, concat_axis=0, tiled=True
    )
    conv_sum, conv_bias_sum, table_sum = cnn_backward(
        chars, char_mask, cnn_grad.astype(jnp.float32), char_table, filters, conv_bias
    )
    conv_weight_sum = jnp.where(used_taps, conv_sum, jnp.zeros_like(conv_sum))
    gain_grads = jnp.stack([gain_zero, gain_one, gain_two], axis=0)
    shift_grads = jnp.stack([shift_zero, shift_one, shift_two], axis=0)
    small_sums = lax.psum(
        (
            conv_weight_sum,
            conv_bias_sum,
            highway_bias_grad,
            project_bias_grad,
            position_grad,
            gain_grads,
            shift_grads,
            qv_bias_grad,
            out_bias_grad,
            up_bias_grad,
            down_bias_grad,
        ),
        "dp",
    )
    table_total = lax.psum(table_sum, ("dp", "mp"))
    large_sums = (
        lax.psum_scatter(highway_weight_grad, "dp", scatter_dimension=1, tiled=True),
        lax.psum_scatter(project_weight_grad, "dp", scatter_dimension=1, tiled=True),
        lax.psum_scatter(qkv_weight_grad, "dp", scatter_dimension=0, tiled=True),
        lax.psum_scatter(out_weight_grad, "dp", scatter_dimension=1, tiled=True),
        lax.psum_scatter(up_weight_grad, "dp", scatter_dimension=0, tiled=True),
        lax.psum_scatter(down_weight_grad, "dp", scatter_dimension=1, tiled=True),
    )
    return (
        encoded,
        table_total,
        small_sums[0],
        small_sums[1],
        large_sums[0],
        small_sums[2],
        large_sums[1],
        small_sums[3],
        small_sums[4],
        small_sums[5],
        small_sums[6],
        large_sums[2],
        small_sums[7],
        large_sums[3],
        small_sums[8],
        large_sums[4],
        small_sums[9],
        large_sums[5],
        small_sums[10],
    )


def solution(mesh):
    return jax.shard_map(
        on_device,
        mesh=mesh,
        in_specs=(
            P("dp", None),
            P("dp", None),
            P(),
            P("dp", None),
            P(),
            P(None, "mp"),
            P("mp"),
            P(None, None, None, "mp"),
            P(None, None, "mp"),
            P("mp", None),
            P(),
            P(),
            P(),
            P(),
            P(None, None, "mp"),
            P(None, "mp"),
            P("mp", None),
            P(),
            P(None, "mp"),
            P("mp"),
            P("mp", None),
            P(),
            P("dp", None),
        ),
        out_specs=(
            P("dp", None),
            P(),
            P(None, "mp"),
            P("mp"),
            P(None, "dp", None, "mp"),
            P(None, None, "mp"),
            P("mp", "dp"),
            P(),
            P(),
            P(),
            P(),
            P("dp", None, "mp"),
            P(None, "mp"),
            P("mp", "dp"),
            P(),
            P("dp", "mp"),
            P("mp"),
            P("mp", "dp"),
            P(),
        ),
        check_vma=False,
    )
```

profile of v0, /device:TPU:1, one launch (start us, length us, event | category | flops | bytes accessed | tf_op | source)
XLA Modules:
  0.0 1284.3 jit_solution(14324495220086014799)
XLA Ops:
  11.2 91.2 %while.9 = (s32[]{:T(128)}, bf16[4,128,512]{2,1,0:T(8,128)(2,1)}, s32[4,128,50]{2,1,0:T(8,128)S(1)}, f32[262,16]{1,0:T(8,128)S(1)}, s32[4,128,50]{1,0,2:T(4,128)...) while((s32[]{:T(128)}, bf16[4,128,512]{2,1,0:T(8,128)(2,1)}, s32[4,128,50]{2,1,0:T(8,128)S(1)}, ...), condition=%wide.region_2.4_spmd, body=%wide.region_0.3_spmd.sunk | while | flops 754023168 | bytes 13428925 | solution.py:70
  57.1 12.7 gather_fusion
  133.4 15.0 %all-gather.6.cloned.1.call-done = bf16[512,2048]{1,0:T(8,128)(2,1)} async-done(((bf16[512,512]{1,0:T(8,128)(2,1)}), bf16[512,2048]{1,0:T(8,128)(2,1)}) %all-gather.6.cloned.1.call-update) | async-done | bytes 2097168 | tf_op jit(solution)/shard_map/all_gather | solution.py:235
  155.4 22.5 %all-gather.4.cloned.1.call-done = bf16[512,2048]{1,0:T(8,128)(2,1)} async-done(((bf16[512,512]{1,0:T(8,128)(2,1)}), bf16[512,2048]{1,0:T(8,128)(2,1)}) %all-gather.4.cloned.1.call-update) | async-done | bytes 2097168 | tf_op jit(solution)/shard_map/all_gather | solution.py:235
  189.0 40.1 %all-reduce.16.cloned.1.call-done = f32[512,768]{1,0:T(8,128)} async-done(((f32[512,768]{1,0:T(8,128)}), f32[512,768]{1,0:T(8,128)}) %all-reduce.16.cloned.1.call-update) | async-done | bytes 1572880 | tf_op jit(solution)/shard_map/psum | solution.py:242
  240.0 43.0 %all-reduce.18.cloned.1.call-done = f32[512,768]{1,0:T(8,128)} async-done(((f32[512,768]{1,0:T(8,128)}), f32[512,768]{1,0:T(8,128)}) %all-reduce.18.cloned.1.call-update) | async-done | bytes 1572880 | tf_op jit(solution)/shard_map/psum | solution.py:262
  291.7 42.6 %all-reduce.20.cloned.1.call-done = f32[512,768]{1,0:T(8,128)} async-done(((f32[512,768]{1,0:T(8,128)}), f32[512,768]{1,0:T(8,128)}) %all-reduce.20.cloned.1.call-update) | async-done | bytes 1572880 | tf_op jit(solution)/shard_map/psum | solution.py:270
  348.6 43.0 %all-reduce.22.cloned.1.call-done = f32[512,768]{1,0:T(8,128)} async-done(((f32[512,768]{1,0:T(8,128)}), f32[512,768]{1,0:T(8,128)}) %all-reduce.22.cloned.1.call-update) | async-done | bytes 1572880 | tf_op jit(solution)/shard_map/psum | solution.py:288
  408.1 33.5 %all-reduce.24.cloned.1.call-done = bf16[512,768]{1,0:T(8,128)(2,1)} async-done(((bf16[512,768]{1,0:T(8,128)(2,1)}), bf16[512,768]{1,0:T(8,128)(2,1)}) %all-reduce.24.cloned.1.call-update) | async-done | bytes 786448 | tf_op jit(solution)/shard_map/psum | solution.py:311
  458.0 32.8 %reduce-scatter.11.cloned.1.call-done = bf16[512,512]{1,0:T(8,128)(2,1)} async-done(((bf16[512,2048]{1,0:T(8,128)(2,1)}), bf16[512,512]{1,0:T(8,128)(2,1)}) %reduce-scatter.11.cloned.1.call-update) | async-done | bytes 524304 | tf_op jit(solution)/shard_map/reduce_scatter | solution.py:341
  546.5 14.3 %all-to-all-done.1 = bf16[8,64,512]{2,1,0:T(8,128)(2,1)S(1)} async-done(((bf16[8,64,512]{2,1,0:T(8,128)(2,1)}), bf16[8,64,512]{2,1,0:T(8,128)(2,1)S(1)}, u32[]{:S(2)}, u32[]{:S(2)}) %all-to-all-start.1) | async-done | bytes 524320 | tf_op jit(solution)/shard_map/all_to_all | solution.py:349
  561.9 185.2 %while.20 = (s32[]{:T(128)}, f32[112,512]{1,0:T(8,128)S(1)}, f32[512]{0:T(512)S(1)}, f32[262,16]{0,1:T(8,128)S(1)}, s32[4,128,50]{2,1,0:T(8,128)}, /*index=5*/f3...) while((s32[]{:T(128)}, f32[112,512]{1,0:T(8,128)S(1)}, ...), condition=%wide.region_28.30_spmd.clone, body=%wide.region_26.29_spmd.clone.sunk | while | flops 2569514752 | bytes 49897364 | solution.py:119
  564.6 12.7 gather_fusion.1
  610.7 12.7 gather_fusion.1
  657.1 12.7 gather_fusion.1
  703.3 12.7 gather_fusion.1
  752.4 30.5 %all-reduce.7 = (f32[512]{0:T(512)}, f32[2,2,512]{2,1,0:T(2,128)}, f32[768]{0:T(1024)}, f32[3,768]{1,0:T(4,128)}, f32[3,768]{1,0:T(4,128)}, /*index=5*/f32[2,192...) all-reduce(f32[512]{0:T(512)S(1)} %get-tuple-element.303, ...), channel_id=1, replica_groups=mesh['dp'=8,'mp'=4] {'dp'}, use_global_device_ids=true, to_apply=%region_31.33 | all-reduce | flops 10624 | bytes 84992 | tf_op jit(solution)/shard_map/psum | solution.py:358
  782.8 44.9 %psum.124 = f32[262,16]{0,1:T(8,128)} all-reduce(f32[262,16]{0,1:T(8,128)S(1)} %copy-done.63), channel_id=1, replica_groups=mesh['dp'=8,'mp'=4] {'dp','mp'}, use_global_device_ids=true, to_apply=%region_29.31 | all-reduce | flops 4192 | bytes 33536 | tf_op jit(solution)/shard_map/psum | solution.py:374
  827.7 61.2 %reduce-scatter.15.cloned.1.call-done = f32[2,256,2,512]{3,1,2,0:T(8,128)} async-done(((f32[2,2048,2,512]{3,1,2,0:T(8,128)}), f32[2,256,2,512]{3,1,2,0:T(8,128)}) %reduce-scatter.15.cloned.1.call-update) | async-done | bytes 2097168 | tf_op jit(solution)/shard_map/reduce_scatter | solution.py:376
  893.4 66.3 %reduce-scatter.19.cloned.1.call-done = f32[96,3,192]{2,0,1:T(8,128)} async-done(((f32[768,3,192]{2,0,1:T(8,128)}), f32[96,3,192]{2,0,1:T(8,128)}) %reduce-scatter.19.cloned.1.call-update) | async-done | bytes 221200 | tf_op jit(solution)/shard_map/reduce_scatter | solution.py:378
  959.7 67.7 %reduce-scatter.17.cloned.1.call-done = f32[512,96]{0,1:T(8,128)} async-done(((f32[512,768]{0,1:T(8,128)}), f32[512,96]{0,1:T(8,128)}) %reduce-scatter.17.cloned.1.call-update) | async-done | bytes 196624 | tf_op jit(solution)/shard_map/reduce_scatter | solution.py:377
  1027.4 72.5 %reduce-scatter.23.cloned.1.call-done = f32[768,96]{0,1:T(8,128)} async-done(((f32[768,768]{0,1:T(8,128)}), f32[768,96]{0,1:T(8,128)}) %reduce-scatter.23.cloned.1.call-update) | async-done | bytes 294928 | tf_op jit(solution)/shard_map/reduce_scatter | solution.py:381
  1099.9 72.4 %reduce-scatter.21.cloned.1.call-done = f32[96,768]{1,0:T(8,128)} async-done(((f32[768,768]{1,0:T(8,128)}), f32[96,768]{1,0:T(8,128)}) %reduce-scatter.21.cloned.1.call-update) | async-done | bytes 294928 | tf_op jit(solution)/shard_map/reduce_scatter | solution.py:380
  1172.2 100.6 %all-reduce.26.cloned.1.call-done = (f32[112,512]{1,0:T(8,128)}, f32[512,768]{1,0:T(8,128)}) async-done(((f32[112,512]{1,0:T(8,128)}, f32[512,768]{1,0:T(8,128)}), (f32[112,512]{1,0:T(8,128)}, f32[512,768]{1,0:T(8,128)})) %all-reduce.26.cloned.1.call-update) | async-done | bytes 1802256 | tf_op jit(solution)/shard_map/psum | solution.py:358
  (596 shorter events, 400.9 us)
Async XLA Ops:
  7.2 281.8 %copy-start = (bf16[768,768]{1,0:T(8,128)(2,1)S(1)}, bf16[768,768]{1,0:T(8,128)(2,1)}, u32[]{:S(2)}) copy-start(bf16[768,768]{1,0:T(8,128)(2,1)} %param.49) | copy-start | bytes 3538948
  11.2 97.7 %copy-start.80 = (s32[4096]{0:T(1024)S(1)}, s32[4096]{0:T(1024)}, u32[]{:S(2)}) copy-start(s32[4096]{0:T(1024)} %param.31) | copy-start | bytes 49156
  102.4 19.8 %all-to-all-start = ((bf16[8,64,512]{2,1,0:T(8,128)(2,1)}), bf16[8,64,512]{2,1,0:T(8,128)(2,1)S(1)}, u32[]{:S(2)}, u32[]{:S(2)}) async-start(bf16[8,64,512]{2,1,0:T(8,128)(2,1)} %bitcast.251), calls=%async_computation | async-start | bytes 1048576 | tf_op jit(solution)/shard_map/all_to_all | solution.py:228
  108.8 39.6 %all-gather.6.cloned.1.call-start = ((), (), s32[]{:S(2)}) async-start(), calls=%async_computation.23 | async-start | bytes 2621440 | tf_op jit(solution)/shard_map/all_gather | solution.py:235
  124.9 53.0 %all-gather.4.cloned.1.call-start = ((), (), s32[]{:S(2)}) async-start(), calls=%async_computation.10 | async-start | bytes 2621440 | tf_op jit(solution)/shard_map/all_gather | solution.py:235
  155.1 73.9 %all-reduce.16.cloned.1.call-start = ((), (), s32[]{:S(2)}) async-start(), calls=%async_computation.11 | async-start | bytes 3145728 | tf_op jit(solution)/shard_map/psum | solution.py:242
  186.6 96.4 %all-reduce.18.cloned.1.call-start = ((), (), s32[]{:S(2)}) async-start(), calls=%async_computation.12 | async-start | bytes 3145728 | tf_op jit(solution)/shard_map/psum | solution.py:262
  188.0 95.0 %copy-start.85 = (f32[768]{0:T(1024)}, f32[768]{0:T(1024)S(1)}, u32[]{:S(2)}) copy-start(f32[768]{0:T(1024)S(1)} %get-tuple-element.496) | copy-start | bytes 9220
  240.0 94.3 %all-reduce.20.cloned.1.call-start = ((), (), s32[]{:S(2)}) async-start(), calls=%async_computation.13 | async-start | bytes 3145728 | tf_op jit(solution)/shard_map/psum | solution.py:270
  291.2 100.4 %all-reduce.22.cloned.1.call-start = ((), (), s32[]{:S(2)}) async-start(), calls=%async_computation.14 | async-start | bytes 3145728 | tf_op jit(solution)/shard_map/psum | solution.py:288
  348.5 46.9 %copy-start.69 = (f32[512]{0:T(512)S(1)}, f32[512]{0:T(512)}, u32[]{:S(2)}) copy-start(f32[512]{0:T(512)} %copy-done.68) | copy-start | bytes 6148
  348.6 93.0 %all-reduce.24.cloned.1.call-start = ((), (), s32[]{:S(2)}) async-start(), calls=%async_computation.15 | async-start | bytes 1572864 | tf_op jit(solution)/shard_map/psum | solution.py:311
  407.9 83.0 %reduce-scatter.11.cloned.1.call-start = ((), (), s32[]{:S(2)}) async-start(), calls=%async_computation.16 | async-start | bytes 2621440 | tf_op jit(solution)/shard_map/reduce_scatter | solution.py:341
  458.0 74.9 %reduce-scatter.13.cloned.1.call-start = ((), (), s32[]{:S(2)}) async-start(), calls=%async_computation.17 | async-start | bytes 2621440 | tf_op jit(solution)/shard_map/reduce_scatter | solution.py:341
  501.3 247.9 %reduce-scatter.25.cloned.1.call-start = ((), (), s32[]{:S(2)}) async-start(), calls=%async_computation.24 | async-start | bytes 884736
  503.8 385.1 %reduce-scatter.15.cloned.1.call-start = ((), (), s32[]{:S(2)}) async-start(), calls=%async_computation.18 | async-start | bytes 18874368 | tf_op jit(solution)/shard_map/reduce_scatter | solution.py:376
  517.6 442.1 %reduce-scatter.19.cloned.1.call-start = ((), (), s32[]{:S(2)}) async-start(), calls=%async_computation.20 | async-start | bytes 2654208 | tf_op jit(solution)/shard_map/reduce_scatter | solution.py:378
  521.2 506.2 %reduce-scatter.17.cloned.1.call-start = ((), (), s32[]{:S(2)}) async-start(), calls=%async_computation.19 | async-start | bytes 1769472 | tf_op jit(solution)/shard_map/reduce_scatter | solution.py:377
  524.5 575.3 %reduce-scatter.23.cloned.1.call-start = ((), (), s32[]{:S(2)}) async-start(), calls=%async_computation.22 | async-start | bytes 2654208 | tf_op jit(solution)/shard_map/reduce_scatter | solution.py:381
  537.2 23.6 %all-to-all-start.1 = ((bf16[8,64,512]{2,1,0:T(8,128)(2,1)}), bf16[8,64,512]{2,1,0:T(8,128)(2,1)S(1)}, u32[]{:S(2)}, u32[]{:S(2)}) async-start(bf16[8,64,512]{2,1,0:T(8,128)(2,1)} %bitcast.39), calls=%async_computation.3 | async-start | bytes 1048576 | tf_op jit(solution)/shard_map/all_to_all | solution.py:349
  542.5 629.8 %reduce-scatter.21.cloned.1.call-start = ((), (), s32[]{:S(2)}) async-start(), calls=%async_computation.21 | async-start | bytes 2654208 | tf_op jit(solution)/shard_map/reduce_scatter | solution.py:380
  546.2 726.7 %all-reduce.26.cloned.1.call-start = ((), (), s32[]{:S(2)}) async-start(), calls=%async_computation.25 | async-start | bytes 3604480 | tf_op jit(solution)/shard_map/psum | solution.py:358
  561.9 185.3 %copy-start.65 = (s32[512]{0:T(512)S(1)}, s32[512]{0:T(512)}, u32[]{:S(2)}) copy-start(s32[512]{0:T(512)} %copy-done.64) | copy-start | bytes 6148
  561.9 185.3 %copy-start.102 = (s32[112]{0:T(128)S(1)}, s32[112]{0:T(128)}, u32[]{:S(2)}) copy-start(s32[112]{0:T(128)} %copy-done.101) | copy-start | bytes 1348
  (119 other events, 542.7 us)
Sparse Core Ops, SparseCore 0:
  125.0 23.3 all-gather.5
  155.3 22.5 all-gather.3
  186.7 42.2 all-reduce.15
  240.1 42.8 all-reduce.17
  291.3 42.8 all-reduce.19
  348.7 42.9 all-reduce.21
  408.0 33.5 all-reduce.23
  458.1 32.6 reduce-scatter.10
  501.4 31.3 reduce-scatter.12
  536.0 63.1 reduce-scatter.24
  603.4 285.4 reduce-scatter.14
  892.8 66.8 reduce-scatter.18
  963.7 63.6 reduce-scatter.16
  1031.7 68.0 reduce-scatter.22
  1104.2 68.0 reduce-scatter.20
  1177.4 95.3 all-reduce.25
where the time goes:
time: 1290 us; the launch traced here: 1280 us
  waiting for transfers between devices  741 us (57%)
  local copies, waits for them, and re-layouts  229 us (18%)
  matrix products  133 us (10%)
  blocking collectives  75.3 us (6%)
  other arithmetic  74.5 us (6%)
  between operations  15.7 us (1%)
  starting transfers between devices  13.5 us (1%)
    gather x32, local copies, waits for them, and re-layouts, embed_rows(): jnp.take(char_table, ids_block, axis=0)  135 us
    psum x1, waiting for transfers between devices, on_device(): lax.psum((conv_weight_sum, conv_bias_sum, highway_bias_grad, project_bias...  101 us
    reduce_scatter x1, waiting for transfers between devices, on_device(): lax.psum_scatter(down_weight_grad, 'dp', scatter_dimension=1, tiled=True)  72.5 us
    reduce_scatter x1, waiting for transfers between devices, on_device(): lax.psum_scatter(up_weight_grad, 'dp', scatter_dimension=0, tiled=True)  72.4 us
    reduce_scatter x1, waiting for transfers between devices, on_device(): lax.psum_scatter(project_weight_grad, 'dp', scatter_dimension=1, tiled=True)  67.7 us
    reduce_scatter x1, waiting for transfers between devices, on_device(): lax.psum_scatter(qkv_weight_grad, 'dp', scatter_dimension=0, tiled=True)  66.3 us
    reduce_scatter x1, waiting for transfers between devices, on_device(): lax.psum_scatter(highway_weight_grad, 'dp', scatter_dimension=1, tiled=True)  61.2 us
    psum x1, blocking collectives, on_device(): table_total = lax.psum(table_sum, ('dp', 'mp'))  44.9 us
  transfers between devices with their start and end apart: 18, of which 17 were waited for; matrix products, arithmetic and copies ran while one was open for 19% of the time, Pallas kernels for 0%

commit v1 on v0

v1 whole, which is shorter than its diff:
```python
import jax
import jax.numpy as jnp
from jax import lax
from jax.sharding import PartitionSpec as P

HEAD = 64
CHANNELS = 2048
CHAR_DIM = 16
CHARS = 50
TAPS = 7
LAYERS = 2

HIGH = lax.Precision.HIGHEST
EPSILON = 1e-05
NEGATIVE = -1e30
F32 = jnp.float32
BF16 = jnp.bfloat16


def filter_mask(local_count, first):
    channel = first + jnp.arange(local_count, dtype=jnp.int32)
    tap_count = 1 + sum(
        ((channel >= CHANNELS // divisor).astype(jnp.int32) for divisor in (64, 32, 16, 8, 4, 2))
    )
    tap_index = jnp.arange(TAPS * CHAR_DIM, dtype=jnp.int32) // CHAR_DIM
    return tap_index[:, None] < tap_count[None, :]


def char_windows(embedded):
    padded = jnp.pad(embedded, ((0, 0), (0, TAPS - 1), (0, 0)))
    return jnp.concatenate(
        [padded[:, offset : offset + CHARS, :] for offset in range(TAPS)], axis=2
    )


def layer_norm(values, gain_row, bias_row):
    center = values - jnp.mean(values, axis=-1, keepdims=True)
    spread = jnp.mean(center * center, axis=-1, keepdims=True)
    return center * lax.rsqrt(spread + EPSILON) * gain_row + bias_row


def embed_rows(ids_block, char_table, filters, conv_bias):
    embedded = (
        jnp.take(char_table, jnp.maximum(ids_block, 0), axis=0)
        * (ids_block >= 0)[..., None].astype(F32)
    ).astype(BF16)
    windows = char_windows(embedded)
    conv_out = jnp.einsum("npk,kc->npc", windows, filters, preferred_element_type=F32) + conv_bias
    return (windows, conv_out)


def pool_conv(conv_out):
    return jnp.mean(jax.nn.silu(conv_out), axis=1)


def cnn_forward(ids_all, char_table, filters, conv_bias):
    def one_block(ids_block):
        return pool_conv(embed_rows(ids_block, char_table, filters, conv_bias)[1])

    pooled = lax.map(one_block, ids_all.reshape(-1, 128, CHARS))
    return pooled.reshape(ids_all.shape[0], -1)


def cnn_backward(ids_all, pooled_grad, char_table, filters, conv_bias):
    block_words = 128
    vocab_ids = jnp.arange(char_table.shape[0], dtype=jnp.int32)

    def one_block(totals, pieces):
        ids_block, grad_block = pieces
        windows, conv_out = embed_rows(ids_block, char_table, filters, conv_bias)
        _, undo = jax.vjp(pool_conv, conv_out)
        conv_grad = undo(grad_block)[0].astype(BF16)
        weight_sum = totals[0] + jnp.einsum(
            "npk,npc->kc", windows, conv_grad, preferred_element_type=F32
        )
        bias_sum = totals[1] + jnp.sum(conv_grad.astype(F32), axis=(0, 1))
        window_grad = jnp.einsum("npc,kc->npk", conv_grad, filters, preferred_element_type=F32)
        window_grad = window_grad.reshape(block_words, CHARS, TAPS, CHAR_DIM)
        padded = jnp.pad(window_grad, ((0, 0), (TAPS - 1, 0), (0, 0), (0, 0)))
        embed_grad = sum(
            (
                padded[:, TAPS - 1 - offset : TAPS - 1 - offset + CHARS, offset, :]
                for offset in range(TAPS)
            )
        )
        onehot = (ids_block.reshape(-1)[:, None] == vocab_ids[None, :]).astype(F32)
        table_sum = totals[2] + jnp.einsum(
            "mv,me->ve", onehot, embed_grad.reshape(-1, CHAR_DIM), precision=HIGH
        )
        return ((weight_sum, bias_sum, table_sum), None)

    local_count = filters.shape[1]
    start_totals = (
        jnp.zeros(filters.shape, F32),
        jnp.zeros((local_count,), F32),
        jnp.zeros(char_table.shape, F32),
    )
    pieces = (
        ids_all.reshape(-1, block_words, CHARS),
        pooled_grad.reshape(-1, block_words, local_count),
    )
    totals, _ = lax.scan(one_block, start_totals, pieces)
    return totals


def highway_mix(both_parts, carried):
    opened = jax.nn.sigmoid(both_parts[:, 1])
    return opened * jax.nn.silu(both_parts[:, 0]) + (1.0 - opened) * carried


def column_sum(values):
    return jnp.sum(values.astype(F32), axis=0)


def swap(values, axis, bit):
    count = lax.axis_size(axis)
    return lax.ppermute(values, axis, [(i, i ^ bit) for i in range(count)])


def bit_reversed(count):
    bits = count.bit_length() - 1
    return [sum(((i >> b) & 1) << (bits - 1 - b) for b in range(bits)) for i in range(count)]


def blocks_by_peer(values, axis, order, count):
    size = values.shape[axis] // count
    me = lax.axis_index("dp")
    return [lax.dynamic_slice_in_dim(values, (me ^ r) * size, size, axis) for r in order]


def halve(blocks, bits, final=F32):
    for bit in bits:
        half = blocks.shape[0] // 2
        got = swap(blocks[half:], "dp", bit)
        blocks = blocks[:half].astype(F32) + got.astype(F32)
        if half > 1:
            blocks = blocks.astype(BF16)
    return blocks[0]


def on_device(
    chars,
    char_mask,
    word_order,
    segment_ids,
    char_table,
    conv_weight,
    conv_bias,
    highway_weight,
    highway_bias,
    project_weight,
    project_bias,
    position_table,
    norm_gain,
    norm_bias,
    qkv_weight,
    qv_bias,
    out_weight,
    out_bias,
    up_weight,
    up_bias,
    down_weight,
    down_bias,
    out_grad,
):
    dp_count = lax.axis_size("dp")
    dp_index = lax.axis_index("dp")
    mp_index = lax.axis_index("mp")
    low = mp_index & 1
    word_count = chars.shape[0]
    per_peer = word_count // dp_count
    half_count = word_count // 2
    local_channels = conv_weight.shape[1]
    dp_bits = [1 << b for b in range(dp_count.bit_length() - 1)]
    order = bit_reversed(dp_count)

    local_rows = (
        lax.dynamic_slice(
            word_order.reshape(dp_count, dp_count, per_peer),
            (0, dp_index, 0),
            (dp_count, 1, per_peer),
        ).reshape(word_count)
        - dp_index * word_count
    )
    places = local_rows ^ (low * half_count)
    perm = (jnp.arange(word_count, dtype=jnp.int32)[:, None] == places[None, :]).astype(BF16)

    def own_half(values):
        return lax.dynamic_slice_in_dim(values, low * half_count, half_count, 0)

    ids = jnp.where(char_mask > 0, chars, -1).reshape(dp_count, per_peer * CHARS)
    ids = lax.all_to_all(ids, "dp", split_axis=0, concat_axis=0, tiled=True)
    ids = ids.reshape(word_count, CHARS)

    used_taps = filter_mask(local_channels, mp_index * local_channels)
    filters = jnp.where(used_taps, conv_weight, jnp.zeros_like(conv_weight))
    pooled = cnn_forward(ids, char_table, filters, conv_bias).astype(BF16)

    def weight_part(depth, r):
        rows = lax.dynamic_slice_in_dim(
            highway_weight[depth], (mp_index ^ r) * local_channels, local_channels, 0
        )
        return rows.reshape(local_channels, -1)

    carried = pooled.astype(F32)
    inputs = pooled
    kept = []
    for depth in range(LAYERS):
        a = inputs
        b = swap(a, "mp", 1)
        c = swap(a, "mp", 2)
        d = swap(c, "mp", 1)
        both = sum(
            jnp.dot(piece, weight_part(depth, r), preferred_element_type=F32)
            for r, piece in enumerate((a, b, c, d))
        )
        both = both.reshape(word_count, 2, local_channels) + highway_bias[depth]
        whole = jnp.zeros((word_count, CHANNELS), BF16)
        for r, piece in enumerate((a, b, c, d)):
            whole = lax.dynamic_update_slice(
                whole, piece, (0, (mp_index ^ r) * local_channels)
            )
        blocks = blocks_by_peer(whole, 1, order, dp_count)
        ours = jnp.concatenate(blocks[: dp_count // 2], axis=1)
        theirs = swap(jnp.concatenate(blocks[dp_count // 2 :], axis=1), "dp", 1)
        kept.append((carried, both, ours, theirs))
        carried = highway_mix(both, carried)
        inputs = carried.astype(BF16)

    def sum_halves(rows, matrix, transposed=False):
        def product(part):
            if transposed:
                return jnp.einsum("nf,df->nd", part, matrix, preferred_element_type=F32)
            return jnp.dot(part, matrix, preferred_element_type=F32)

        got = swap(product(rows[half_count:]), "mp", 1)
        pair = (product(rows[:half_count]) + got).astype(BF16)
        return pair.astype(F32) + swap(pair, "mp", 2).astype(F32)

    def both_halves(values):
        return jnp.concatenate([values, swap(values, "mp", 1)], axis=0)

    state = jnp.dot(perm, inputs, preferred_element_type=F32).astype(BF16)
    embed_total = sum_halves(state, project_weight) + project_bias + own_half(position_table)
    hidden_in = layer_norm(embed_total, norm_gain[0], norm_bias[0])
    x_low = both_halves(hidden_in.astype(BF16))
    qkv_out = jnp.einsum("nd,djh->njh", x_low, qkv_weight, preferred_element_type=F32)
    heads = qkv_weight.shape[2] // HEAD
    head_shape = (word_count, heads, HEAD)
    query = (qkv_out[:, 0] + qv_bias[0]).astype(BF16).reshape(head_shape)
    keys = qkv_out[:, 1].astype(BF16).reshape(head_shape)
    values = (qkv_out[:, 2] + qv_bias[1]).astype(BF16).reshape(head_shape)
    segments = segment_ids[0]
    segments = jnp.where(low > 0, jnp.roll(segments, half_count), segments)
    same_doc = segments[:, None] == segments[None, :]
    scale = HEAD ** (-0.5)
    scores = jnp.einsum("qhe,khe->hqk", query, keys, preferred_element_type=F32) * scale
    scores = jnp.where(same_doc[None], scores, NEGATIVE)
    exps = jnp.exp(scores - jnp.max(scores, axis=-1, keepdims=True))
    probs = exps / jnp.sum(exps, axis=-1, keepdims=True)
    probs_low = probs.astype(BF16)
    mixed = jnp.einsum("hqk,khe->qhe", probs_low, values, preferred_element_type=F32)
    mixed = mixed.astype(BF16).reshape(word_count, -1)
    resid_one = hidden_in + sum_halves(mixed, out_weight) + out_bias
    hidden_mid = layer_norm(resid_one, norm_gain[1], norm_bias[1])
    mid_low = both_halves(hidden_mid.astype(BF16))
    upward = jnp.dot(mid_low, up_weight, preferred_element_type=F32) + up_bias
    activated = jax.nn.gelu(upward).astype(BF16)
    resid_two = hidden_mid + sum_halves(activated, down_weight) + down_bias
    encoded = layer_norm(resid_two, norm_gain[2], norm_bias[2])

    _, undo = jax.vjp(layer_norm, resid_two, norm_gain[2], norm_bias[2])
    resid_two_grad, gain_two, shift_two = undo(own_half(out_grad))
    down_low = resid_two_grad.astype(BF16)
    down_bias_grad = column_sum(down_low)
    down_grad = both_halves(down_low)
    act_grad = jnp.einsum("nd,fd->nf", down_grad, down_weight, preferred_element_type=F32)
    _, undo = jax.vjp(jax.nn.gelu, upward)
    up_grad = undo(act_grad)[0].astype(BF16)
    mid_grad = resid_two_grad + sum_halves(up_grad, up_weight, True)
    up_bias_grad = column_sum(up_grad)
    down_weight_grad = jnp.einsum("nd,nf->df", down_grad, activated, preferred_element_type=F32)
    up_weight_grad = jnp.einsum("nd,nf->df", mid_low, up_grad, preferred_element_type=F32)
    _, undo = jax.vjp(layer_norm, resid_one, norm_gain[1], norm_bias[1])
    resid_one_grad, gain_one, shift_one = undo(mid_grad)
    attn_low = resid_one_grad.astype(BF16)
    out_bias_grad = column_sum(attn_low)
    attn_grad = both_halves(attn_low)
    mixed_grad = jnp.einsum("nd,hd->nh", attn_grad, out_weight, preferred_element_type=F32)
    mixed_grad = mixed_grad.astype(BF16).reshape(head_shape)
    out_weight_grad = jnp.einsum("nd,nh->dh", attn_grad, mixed, preferred_element_type=F32)
    prob_grad = jnp.einsum("qhe,khe->hqk", mixed_grad, values, preferred_element_type=F32)
    score_grad = (
        probs * (prob_grad - jnp.sum(probs * prob_grad, axis=-1, keepdims=True))
    ).astype(BF16)
    query_grad = jnp.einsum("hqk,khe->qhe", score_grad, keys, preferred_element_type=F32) * scale
    key_grad = jnp.einsum("hqk,qhe->khe", score_grad, query, preferred_element_type=F32) * scale
    value_grad = jnp.einsum("hqk,qhe->khe", probs_low, mixed_grad, preferred_element_type=F32)
    qkv_grad = jnp.concatenate(
        [g.astype(BF16).reshape(word_count, -1) for g in (query_grad, key_grad, value_grad)],
        axis=1,
    )
    qkv_flat = qkv_weight.reshape(qkv_weight.shape[0], -1)
    hidden_grad = resid_one_grad + sum_halves(qkv_grad, qkv_flat, True)
    local_heads = qkv_weight.shape[2]
    qkv_sums = column_sum(qkv_grad)
    qv_bias_grad = jnp.stack([qkv_sums[:local_heads], qkv_sums[2 * local_heads :]], axis=0)
    qkv_weight_grad = jnp.einsum("nd,nh->dh", x_low, qkv_grad, preferred_element_type=F32)
    _, undo = jax.vjp(layer_norm, embed_total, norm_gain[0], norm_bias[0])
    embed_grad, gain_zero, shift_zero = undo(hidden_grad)
    proj_low = embed_grad.astype(BF16)
    project_bias_grad = column_sum(proj_low)
    proj_grad = both_halves(proj_low)
    proj_words = jnp.einsum("tw,td->wd", perm, proj_grad, preferred_element_type=F32).astype(BF16)
    state_grad = jnp.einsum("nd,cd->nc", proj_words, project_weight, preferred_element_type=F32)
    project_weight_grad = jnp.einsum(
        "nd,nc->dc", proj_words, inputs, preferred_element_type=F32
    )
    encoder_grads = jnp.concatenate(
        [qkv_weight_grad, out_weight_grad, up_weight_grad, down_weight_grad, project_weight_grad],
        axis=1,
    )
    encoder_blocks = jnp.stack(blocks_by_peer(encoder_grads, 0, order, dp_count), axis=0)
    encoder_sum = halve(encoder_blocks.astype(BF16), dp_bits)

    level_sums = [None] * LAYERS
    level_bias_grads = [None] * LAYERS
    for depth in reversed(range(LAYERS)):
        carried_now, both_now, ours, theirs = kept[depth]
        _, undo = jax.vjp(highway_mix, both_now, carried_now)
        both_grad, carried_grad = undo(state_grad)
        both_low = both_grad.astype(BF16).reshape(word_count, -1)
        level_bias_grads[depth] = column_sum(both_low).reshape(2, local_channels)
        parts = [
            jnp.einsum(
                "nf,kf->nk", both_low, weight_part(depth, r), preferred_element_type=F32
            )
            for r in (3, 2, 1, 0)
        ]
        far = (parts[1] + swap(parts[0].astype(BF16), "mp", 1).astype(F32)).astype(BF16)
        near = parts[3] + swap(parts[2].astype(BF16), "mp", 1).astype(F32)
        state_grad = near + swap(far, "mp", 2).astype(F32) + carried_grad
        peer_grad = swap(both_low, "dp", 1)
        weight_grad = jnp.einsum("nk,nf->kf", ours, both_low, preferred_element_type=F32)
        weight_grad += jnp.einsum("nk,nf->kf", theirs, peer_grad, preferred_element_type=F32)
        weight_grad = weight_grad.astype(BF16).reshape(
            dp_count // 2, CHANNELS // dp_count, 2 * local_channels
        )
        level_sums[depth] = halve(weight_grad, dp_bits[1:]).reshape(-1, 2, local_channels)
    highway_weight_grad = jnp.stack(level_sums, axis=0)
    highway_bias_grad = jnp.stack(level_bias_grads, axis=0)
    pooled_grad = state_grad.astype(BF16).astype(F32)

    conv_sum, conv_bias_sum, table_sum = cnn_backward(
        ids, pooled_grad, char_table, filters, conv_bias
    )
    conv_weight_sum = jnp.where(used_taps, conv_sum, jnp.zeros_like(conv_sum))

    def over_dp(values):
        for bit in dp_bits:
            values = values + swap(values, "dp", bit)
        return values

    def pack(items):
        return jnp.concatenate([item.reshape(-1) for item in items]).reshape(-1, 128)

    def unpack(packed, items):
        flat = packed.reshape(-1)
        result, first = [], 0
        for item in items:
            result.append(flat[first : first + item.size].reshape(item.shape))
            first += item.size
        return result

    row_items = [
        project_bias_grad,
        jnp.stack([gain_zero, gain_one, gain_two], axis=0),
        jnp.stack([shift_zero, shift_one, shift_two], axis=0),
        out_bias_grad,
        down_bias_grad,
    ]
    row_pack = pack(row_items)
    row_pack = row_pack + swap(row_pack, "mp", 1)
    shard_items = [highway_bias_grad, qv_bias_grad, up_bias_grad]
    small = over_dp(jnp.concatenate([row_pack, pack(shard_items)], axis=0))
    row_sums = unpack(small[: row_pack.shape[0]], row_items)
    shard_sums = unpack(small[row_pack.shape[0] :], shard_items)

    position_half = over_dp(embed_grad)
    position_grad = both_halves(position_half)

    conv_items = [conv_weight_sum, conv_bias_sum]
    conv_pack = pack(conv_items)
    conv_sums = unpack(over_dp(conv_pack), conv_items)
    table_total = table_sum
    table_total = table_total + swap(table_total, "mp", 1)
    table_total = table_total + swap(table_total, "mp", 2)
    table_total = over_dp(table_total)

    def in_order(values):
        first, second = values[:half_count], values[half_count:]
        return jnp.concatenate(
            [jnp.where(low > 0, second, first), jnp.where(low > 0, first, second)], axis=0
        )

    bounds, first = [], 0
    for width in (3 * local_heads, local_heads, up_weight.shape[1], down_weight.shape[0], local_channels):
        bounds.append(encoder_sum[:, first : first + width])
        first += width
    return (
        in_order(both_halves(encoded)),
        table_total,
        conv_sums[0],
        conv_sums[1],
        highway_weight_grad,
        shard_sums[0],
        bounds[4].T,
        row_sums[0],
        in_order(position_grad),
        row_sums[1],
        row_sums[2],
        bounds[0].reshape(-1, 3, local_heads),
        shard_sums[1],
        bounds[1].T,
        row_sums[3],
        bounds[2],
        shard_sums[2],
        bounds[3].T,
        row_sums[4],
    )


def solution(mesh):
    return jax.shard_map(
        on_device,
        mesh=mesh,
        in_specs=(
            P("dp", None),
            P("dp", None),
            P(),
            P("dp", None),
            P(),
            P(None, "mp"),
            P("mp"),
            P(None, None, None, "mp"),
            P(None, None, "mp"),
            P("mp", None),
            P(),
            P(),
            P(),
            P(),
            P(None, None, "mp"),
            P(None, "mp"),
            P("mp", None),
            P(),
            P(None, "mp"),
            P("mp"),
            P("mp", None),
            P(),
            P("dp", None),
        ),
        out_specs=(
            P("dp", None),
            P(),
            P(None, "mp"),
            P("mp"),
            P(None, "dp", None, "mp"),
            P(None, None, "mp"),
            P("mp", "dp"),
            P(),
            P(),
            P(),
            P(),
            P("dp", None, "mp"),
            P(None, "mp"),
            P("mp", "dp"),
            P(),
            P("dp", "mp"),
            P("mp"),
            P("mp", "dp"),
            P(),
        ),
        check_vma=False,
    )
```

time: 1290 us -> 773 us (0.60)
  waiting for transfers between devices: 741 us -> 188 us
  blocking collectives: 75.3 us -> 0 us
  starting transfers between devices: 13.5 us -> 60.7 us
  local copies, waits for them, and re-layouts: 229 us -> 266 us
  matrix products: 133 us -> 153 us
  between operations: 15.7 us -> 2.71 us
    reduce_scatter x7 -> x0, waiting for transfers between devices: 376 us -> none  [the longest x1 72.5 us: on_device(): lax.psum_scatter(down_weight_grad, 'dp', scatter_dimension=1, tiled=True)]
    psum x6 -> x0, waiting for transfers between devices: 303 us -> none  [the longest x1 101 us: on_device(): lax.psum((conv_weight_sum, conv_bias_sum, highway_bias_grad, project_bias...]
    ppermute x0 -> x55, waiting for transfers between devices: none -> 188 us  [swap(): return lax.ppermute(values, axis, [(i, i ^ bit) for i in range(count)])]
    psum x2 -> x0, blocking collectives: 75.3 us -> none  [the longest x1 44.9 us: on_device(): table_total = lax.psum(table_sum, ('dp', 'mp'))]
    ppermute x0 -> x55, starting transfers between devices: none -> 54.3 us  [swap(): return lax.ppermute(values, axis, [(i, i ^ bit) for i in range(count)])]
    all_gather x2 -> x0, waiting for transfers between devices: 37.4 us -> none  [on_device(): lax.all_gather(inputs, 'mp', axis=1, tiled=True)]
    all_to_all x2 -> x1, waiting for transfers between devices: 25 us -> 0.01 us  [on_device(): ids = lax.all_to_all(ids, 'dp', split_axis=0, concat_axis=0, tiled=True)]
    dot_general x41 -> x62, matrix products: 118 us -> 135 us  [the longest x8 42.3 us: embed_rows(): jnp.einsum('npk,kc->npc', windows, filters, preferred_element_type=F32)]
  transfers between devices with their start and end apart: 18 -> 56, of which waited for: 17 -> 26; matrix products, arithmetic and copies ran while one was open for 19% -> 47% of each run, Pallas kernels for 0% -> 0%
where the time goes in v1:
time: 773 us; the launch traced here: 760 us
  local copies, waits for them, and re-layouts  266 us (34%)
  waiting for transfers between devices  188 us (24%)
  matrix products  153 us (20%)
  other arithmetic  87.2 us (11%)
  starting transfers between devices  60.7 us (8%)
    ppermute x55, waiting for transfers between devices, swap(): return lax.ppermute(values, axis, [(i, i ^ bit) for i in range(count)])  188 us
    gather x32, local copies, waits for them, and re-layouts, embed_rows(): jnp.take(char_table, jnp.maximum(ids_block, 0), axis=0)  135 us
    ppermute x55, starting transfers between devices, swap(): return lax.ppermute(values, axis, [(i, i ^ bit) for i in range(count)])  54.3 us
    dot_general x8, matrix products, embed_rows(): jnp.einsum('npk,kc->npc', windows, filters, preferred_element_type=F32)  42.3 us
    unnamed x247, local copies, waits for them, and re-layouts  26.3 us
    reshape x4, local copies, waits for them, and re-layouts, one_block(): window_grad = window_grad.reshape(block_words, CHARS, TAPS, CHAR_DIM)  24.9 us
    add x4, other arithmetic, one_block(): sum((padded[:, TAPS - 1 - offset:TAPS - 1 - offset + CHARS, offset, :] fo...  19.2 us
    dot_general x4, matrix products, one_block(): jnp.einsum('npk,npc->kc', windows, conv_grad, preferred_element_type=F32)  15.9 us
  transfers between devices with their start and end apart: 56, of which 26 were waited for; matrix products, arithmetic and copies ran while one was open for 47% of the time, Pallas kernels for 0%

profile of v1, /device:TPU:1, one launch (start us, length us, event | category | flops | bytes accessed | tf_op | source)
XLA Modules:
  0.0 759.9 jit_solution(2236328893818663969)
XLA Ops:
  9.3 8.4 %fusion.161 = (bf16[1,2048,2,512]{3,2,1,0:T(2,128)(2,1)}, bf16[1,2048,2,512]{3,2,1,0:T(2,128)(2,1)}) fusion(bf16[2,2048,2,512]{3,2,1,0:T(2,128)(2,1)} %param.36), kind=kLoop, calls=%fused_computation.408 | loop fusion | bytes 16777216 | tf_op jit(solution)/shard_map/slice | solution.py:201
  39.0 90.3 %while.29 = (s32[]{:T(128)}, bf16[4,128,512]{2,1,0:T(8,128)(2,1)}, s32[4,128,50]{2,1,0:T(8,128)S(1)}, f32[262,16]{1,0:T(8,128)S(1)}, bf16[112,512]{1,0:T(8,128)(2,1)S(1)}, /*index=5*/f32[512]{0:T(512)S(1)}, s32[]{:T(128)}) while((s32[]{:T(128)}, bf16[4,128,512]{2,1,0:T(8,128)(2,1)}, s32[4,128,50]{2,1,0:T(8,128)S(1)}, f32[262,16]{1,0:T(8,128)S(1)}, ...), condition=%wide.region_2.4_spmd, body=%wide.region_0.3_spmd.sunk | while | flops 754035968 | bytes 13420689 | solution.py:60
  39.2 12.7 %gather_fusion = f32[6400,16]{1,0:T(8,128)} fusion(f32[262,16]{1,0:T(8,128)S(1)} %get-tuple-element.691, s32[7168]{0:T(1024)S(1)} %pad_clamp_fusion.4), kind=kCustom, calls=%fused_computation.clone.clone.1 | custom fusion | bytes 844800 | tf_op jit(solution)/shard_map/while/body/eval_jaxpr/jit(_take)/gather | solution.py:44
  61.7 12.7 %gather_fusion = f32[6400,16]{1,0:T(8,128)} fusion(f32[262,16]{1,0:T(8,128)S(1)} %get-tuple-element.691, s32[7168]{0:T(1024)S(1)} %pad_clamp_fusion.4), kind=kCustom, calls=%fused_computation.clone.clone.1 | custom fusion | bytes 844800 | tf_op jit(solution)/shard_map/while/body/eval_jaxpr/jit(_take)/gather | solution.py:44
  84.3 12.7 %gather_fusion = f32[6400,16]{1,0:T(8,128)} fusion(f32[262,16]{1,0:T(8,128)S(1)} %get-tuple-element.691, s32[7168]{0:T(1024)S(1)} %pad_clamp_fusion.4), kind=kCustom, calls=%fused_computation.clone.clone.1 | custom fusion | bytes 844800 | tf_op jit(solution)/shard_map/while/body/eval_jaxpr/jit(_take)/gather | solution.py:44
  106.8 12.7 %gather_fusion = f32[6400,16]{1,0:T(8,128)} fusion(f32[262,16]{1,0:T(8,128)S(1)} %get-tuple-element.691, s32[7168]{0:T(1024)S(1)} %pad_clamp_fusion.4), kind=kCustom, calls=%fused_computation.clone.clone.1 | custom fusion | bytes 844800 | tf_op jit(solution)/shard_map/while/body/eval_jaxpr/jit(_take)/gather | solution.py:44
  135.4 7.9 %collective-permute-done.1 = bf16[512,512]{0,1:T(8,128)(2,1)S(1)} collective-permute-done((bf16[512,512]{0,1:T(8,128)(2,1)S(1)}, bf16[512,512]{0,1:T(8,128)(2,1)S(1)}, u32[]{:S(2)}, u32[]{:S(2)}) %collective-permute-start.1) | collective-permute-done | bytes 524320 | tf_op jit(solution)/shard_map/ppermute | solution.py:117
  187.8 9.4 %collective-permute-done.7 = bf16[256,768]{1,0:T(8,128)(2,1)} collective-permute-done((bf16[256,768]{1,0:T(8,128)(2,1)}, bf16[256,768]{1,0:T(8,128)(2,1)}, u32[]{:S(2)}, u32[]{:S(2)}) %collective-permute-start.7) | collective-permute-done | bytes 393248 | tf_op jit(solution)/shard_map/ppermute | solution.py:117
  214.9 9.1 %collective-permute-done.10 = bf16[256,768]{1,0:T(8,128)(2,1)S(1)} collective-permute-done((bf16[256,768]{1,0:T(8,128)(2,1)S(1)}, bf16[256,768]{1,0:T(8,128)(2,1)S(1)}, u32[]{:S(2)}, u32[]{:S(2)}) %collective-permute-start.10) | collective-permute-done | bytes 393248 | tf_op jit(solution)/shard_map/ppermute | solution.py:117
  234.3 9.1 %collective-permute-done.13 = bf16[256,768]{1,0:T(8,128)(2,1)S(1)} collective-permute-done((bf16[256,768]{1,0:T(8,128)(2,1)S(1)}, bf16[256,768]{1,0:T(8,128)(2,1)S(1)}, u32[]{:S(2)}, u32[]{:S(2)}) %collective-permute-start.13) | collective-permute-done | bytes 393248 | tf_op jit(solution)/shard_map/ppermute | solution.py:117
  286.9 7.4 collective-permute-done.20
  332.8 15.8 %collective-permute-done.41 = bf16[512,1024]{0,1:T(8,128)(2,1)S(1)} collective-permute-done((bf16[512,1024]{0,1:T(8,128)(2,1)S(1)}, bf16[512,1024]{0,1:T(8,128)(2,1)S(1)}, u32[]{:S(2)}, u32[]{:S(2)}) %collective-permute-start.41) | collective-permute-done | bytes 1048608 | tf_op jit(solution)/shard_map/ppermute | solution.py:117
  368.3 10.0 %collective-permute-done.46 = f32[79,128]{1,0:T(8,128)S(1)} collective-permute-done((f32[79,128]{1,0:T(8,128)S(1)}, f32[79,128]{1,0:T(8,128)S(1)}, u32[]{:S(2)}, u32[]{:S(2)}) %collective-permute-start.46) | collective-permute-done | bytes 40480 | tf_op jit(solution)/shard_map/ppermute | solution.py:117
  391.5 27.7 %collective-permute-done.53 = f32[256,768]{1,0:T(8,128)} collective-permute-done((f32[256,768]{1,0:T(8,128)}, f32[256,768]{1,0:T(8,128)}, u32[]{:S(2)}, u32[]{:S(2)}) %collective-permute-start.53) | collective-permute-done | bytes 786464 | tf_op jit(solution)/shard_map/ppermute | solution.py:117
  440.5 195.3 %while.30 = (s32[]{:T(128)}, f32[112,512]{1,0:T(8,128)S(1)}, f32[512]{0:T(512)S(1)}, f32[262,16]{0,1:T(8,128)S(1)}, s32[4,128,50]{2,1,0:T(8,128)}, /*index=5*/f3...) while((s32[]{:T(128)}, f32[112,512]{1,0:T(8,128)S(1)}, ...), condition=%wide.region_20.22_spmd.clone, body=%wide.region_18.21_spmd.clone.sunk | while | flops 2569431552 | bytes 75906968 | solution.py:102
  441.6 12.7 %gather_fusion.1 = f32[6400,16]{1,0:T(8,128)} fusion(f32[262,16]{1,0:T(8,128)S(1)} %get-tuple-element.722, s32[7168]{0:T(1024)S(1)} %pad_clamp_fusion.5), kind=kCustom, calls=%fused_computation.1.clone.clone.1 | custom fusion | bytes 844800 | tf_op jit(solution)/shard_map/while/body/eval_jaxpr/jit(_take)/gather | solution.py:44
  490.3 12.7 %gather_fusion.1 = f32[6400,16]{1,0:T(8,128)} fusion(f32[262,16]{1,0:T(8,128)S(1)} %get-tuple-element.722, s32[7168]{0:T(1024)S(1)} %pad_clamp_fusion.5), kind=kCustom, calls=%fused_computation.1.clone.clone.1 | custom fusion | bytes 844800 | tf_op jit(solution)/shard_map/while/body/eval_jaxpr/jit(_take)/gather | solution.py:44
  508.8 6.6 convert_reduce_fusion.9
  539.1 12.7 %gather_fusion.1 = f32[6400,16]{1,0:T(8,128)} fusion(f32[262,16]{1,0:T(8,128)S(1)} %get-tuple-element.722, s32[7168]{0:T(1024)S(1)} %pad_clamp_fusion.5), kind=kCustom, calls=%fused_computation.1.clone.clone.1 | custom fusion | bytes 844800 | tf_op jit(solution)/shard_map/while/body/eval_jaxpr/jit(_take)/gather | solution.py:44
  587.9 12.7 %gather_fusion.1 = f32[6400,16]{1,0:T(8,128)} fusion(f32[262,16]{1,0:T(8,128)S(1)} %get-tuple-element.722, s32[7168]{0:T(1024)S(1)} %pad_clamp_fusion.5), kind=kCustom, calls=%fused_computation.1.clone.clone.1 | custom fusion | bytes 844800 | tf_op jit(solution)/shard_map/while/body/eval_jaxpr/jit(_take)/gather | solution.py:44
  606.3 6.6 convert_reduce_fusion.9
  661.8 8.1 %collective-permute-done.32 = f32[262,16]{0,1:T(8,128)S(1)} collective-permute-done((f32[262,16]{0,1:T(8,128)S(1)}, f32[262,16]{0,1:T(8,128)S(1)}, u32[]{:S(2)}, u32[]{:S(2)}) %collective-permute-start.32) | collective-permute-done | bytes 16800 | tf_op jit(solution)/shard_map/ppermute | solution.py:117
  684.9 18.2 %collective-permute-done.35 = f32[452,128]{1,0:T(8,128)} collective-permute-done((f32[452,128]{1,0:T(8,128)}, f32[452,128]{1,0:T(8,128)}, u32[]{:S(2)}, u32[]{:S(2)}) %collective-permute-start.35) | collective-permute-done | bytes 231456 | tf_op jit(solution)/shard_map/ppermute | solution.py:117
  715.5 27.9 %collective-permute-done.39 = bf16[1,256,1024]{2,1,0:T(8,128)(2,1)} collective-permute-done((bf16[1,256,1024]{2,1,0:T(8,128)(2,1)}, bf16[1,256,1024]{2,1,0:T(8,128)(2,1)}, u32[]{:S(2)}, u32[]{:S(2)}) %collective-permute-start.39) | collective-permute-done | bytes 524320 | tf_op jit(solution)/shard_map/ppermute | solution.py:117
  (764 shorter events, 481.9 us)
Async XLA Ops:
  2.8 35.6 %all-to-all-start = ((s32[8,1,3200]{2,1,0:T(1,128)}), s32[8,1,3200]{2,1,0:T(1,128)S(1)}, u32[]{:S(2)}, u32[]{:S(2)}) async-start(s32[8,1,3200]{2,1,0:T(1,128)} %all_to_all.8), calls=%async_computation | async-start | bytes 204800 | tf_op jit(solution)/shard_map/all_to_all | solution.py:192
  132.1 13.9 %collective-permute-start = (bf16[512,512]{0,1:T(8,128)(2,1)S(1)}, bf16[512,512]{0,1:T(8,128)(2,1)S(1)}, u32[]{:S(2)}, u32[]{:S(2)}) collective-permute-start(bf16[512,512]{0,1:T(8,128)(2,1)S(1)} %copy.193), channel_id=1, source_target_pairs={{0,1},{1,0},{2,3},{3,2},{4,5},{5,4},{6,7},{7,6},{8,9},{9,8},{10,11... | collective-permute-start | bytes 1572872 | tf_op jit(solution)/shard_map/ppermute | solution.py:117
  262.6 162.7 %collective-permute-start.36 = (bf16[512,1024]{0,1:T(8,128)(2,1)}, bf16[512,1024]{0,1:T(8,128)(2,1)}, u32[]{:S(2)}, u32[]{:S(2)}) collective-permute-start(bf16[512,1024]{0,1:T(8,128)(2,1)} %pad_maximum_fusion.4), channel_id=1, source_target_pairs={{0,4},{4,0},{8,12},{12,8},{16,20},{20,16},{24,28},{28,24},{1,5},{5... | collective-permute-start | bytes 3145736 | tf_op jit(solution)/shard_map/ppermute | solution.py:117
  267.7 64.9 %collective-permute-start.40 = (bf16[512,1024]{0,1:T(8,128)(2,1)}, bf16[512,1024]{0,1:T(8,128)(2,1)}, u32[]{:S(2)}, u32[]{:S(2)}) collective-permute-start(bf16[512,1024]{0,1:T(8,128)(2,1)} %pad_maximum_fusion.5), channel_id=1, source_target_pairs={{0,4},{4,0},{8,12},{12,8},{16,20},{20,16},{24,28},{28,24},{1,5},{5... | collective-permute-start | bytes 3145736 | tf_op jit(solution)/shard_map/ppermute | solution.py:117
  297.4 28.9 %collective-permute-start.51 = (f32[256,768]{1,0:T(8,128)}, f32[256,768]{1,0:T(8,128)}, u32[]{:S(2)}, u32[]{:S(2)}) collective-permute-start(f32[256,768]{1,0:T(8,128)} %get-tuple-element.458), channel_id=1, source_target_pairs={{0,4},{4,0},{8,12},{12,8},{16,20},{20,16},{24,28},{28,24},{1,5},{5... | collective-permute-start | bytes 2359304 | tf_op jit(solution)/shard_map/ppermute | solution.py:117
  316.2 32.4 %collective-permute-start.41 = (bf16[512,1024]{0,1:T(8,128)(2,1)S(1)}, bf16[512,1024]{0,1:T(8,128)(2,1)S(1)}, u32[]{:S(2)}, u32[]{:S(2)}) collective-permute-start(bf16[512,1024]{0,1:T(8,128)(2,1)S(1)} %bitcast.377), channel_id=1, source_target_pairs={{0,4},{4,0},{8,12},{12,8},{16,20},{20,16},{24,28},{28,24},{1,5},{5... | collective-permute-start | bytes 3145736 | tf_op jit(solution)/shard_map/ppermute | solution.py:117
  326.3 29.2 %collective-permute-start.22 = (bf16[512,512]{0,1:T(8,128)(2,1)S(1)}, bf16[512,512]{0,1:T(8,128)(2,1)S(1)}, u32[]{:S(2)}, u32[]{:S(2)}) collective-permute-start(bf16[512,512]{0,1:T(8,128)(2,1)S(1)} %convolution_convert_fusion.5), channel_id=1, source_target_pairs={{0,1},{1,0},{2,3},{3,2},{4,5},{5,4},{6,7},{7,6},{8,9},{9,8},{10,11... | collective-permute-start | bytes 1572872 | tf_op jit(solution)/shard_map/ppermute | solution.py:117
  330.2 50.5 %collective-permute-start.52 = (f32[256,768]{1,0:T(8,128)S(1)}, f32[256,768]{1,0:T(8,128)S(1)}, u32[]{:S(2)}, u32[]{:S(2)}) collective-permute-start(f32[256,768]{1,0:T(8,128)S(1)} %add.756), channel_id=1, source_target_pairs={{0,8},{4,12},{8,0},{12,4},{16,24},{20,28},{24,16},{28,20},{1,9},{5... | collective-permute-start | bytes 2359304 | tf_op jit(solution)/shard_map/ppermute | solution.py:117
  332.5 23.0 %collective-permute-start.24 = (bf16[512,512]{0,1:T(8,128)(2,1)S(1)}, bf16[512,512]{0,1:T(8,128)(2,1)S(1)}, u32[]{:S(2)}, u32[]{:S(2)}) collective-permute-start(bf16[512,512]{0,1:T(8,128)(2,1)S(1)} %add_convert_fusion.7), channel_id=1, source_target_pairs={{0,2},{1,3},{2,0},{3,1},{4,6},{5,7},{6,4},{7,5},{8,10},{9,11},{10,... | collective-permute-start | bytes 1572872 | tf_op jit(solution)/shard_map/ppermute | solution.py:117
  354.1 68.6 %collective-permute-start.42 = (bf16[2,256,1024]{2,1,0:T(8,128)(2,1)}, bf16[2,256,1024]{2,1,0:T(8,128)(2,1)}, u32[]{:S(2)}, u32[]{:S(2)}) collective-permute-start(bf16[2,256,1024]{2,1,0:T(8,128)(2,1)} %bitcast.47), channel_id=1, source_target_pairs={{0,8},{4,12},{8,0},{12,4},{16,24},{20,28},{24,16},{28,20},{1,9},{5... | collective-permute-start | bytes 3145736 | tf_op jit(solution)/shard_map/ppermute | solution.py:117
  362.4 16.0 %collective-permute-start.46 = (f32[79,128]{1,0:T(8,128)S(1)}, f32[79,128]{1,0:T(8,128)S(1)}, u32[]{:S(2)}, u32[]{:S(2)}) collective-permute-start(f32[79,128]{1,0:T(8,128)S(1)} %fusion.256), channel_id=1, source_target_pairs={{0,8},{4,12},{8,0},{12,4},{16,24},{20,28},{24,16},{28,20},{1,9},{5... | collective-permute-start | bytes 121352 | tf_op jit(solution)/shard_map/ppermute | solution.py:117
  366.2 22.9 %collective-permute-start.26 = (bf16[512,512]{0,1:T(8,128)(2,1)}, bf16[512,512]{0,1:T(8,128)(2,1)}, u32[]{:S(2)}, u32[]{:S(2)}) collective-permute-start(bf16[512,512]{0,1:T(8,128)(2,1)} %convolution_convert_fusion.2), channel_id=1, source_target_pairs={{0,1},{1,0},{2,3},{3,2},{4,5},{5,4},{6,7},{7,6},{8,9},{9,8},{10,11... | collective-permute-start | bytes 1572872 | tf_op jit(solution)/shard_map/ppermute | solution.py:117
  381.7 37.5 %collective-permute-start.53 = (f32[256,768]{1,0:T(8,128)}, f32[256,768]{1,0:T(8,128)}, u32[]{:S(2)}, u32[]{:S(2)}) collective-permute-start(f32[256,768]{1,0:T(8,128)} %add.757), channel_id=1, source_target_pairs={{0,16},{4,20},{8,24},{12,28},{16,0},{20,4},{24,8},{28,12},{1,17},{... | collective-permute-start | bytes 2359304 | tf_op jit(solution)/shard_map/ppermute | solution.py:117
  384.5 41.1 %collective-permute-start.37 = (bf16[512,1024]{0,1:T(8,128)(2,1)}, bf16[512,1024]{0,1:T(8,128)(2,1)}, u32[]{:S(2)}, u32[]{:S(2)}) collective-permute-start(bf16[512,1024]{0,1:T(8,128)(2,1)} %bitcast.40), channel_id=1, source_target_pairs={{0,4},{4,0},{8,12},{12,8},{16,20},{20,16},{24,28},{28,24},{1,5},{5... | collective-permute-start | bytes 3145736 | tf_op jit(solution)/shard_map/ppermute | solution.py:117
  389.1 258.6 %collective-permute-start.48 = (bf16[4,96,2816]{2,1,0:T(8,128)(2,1)}, bf16[4,96,2816]{2,1,0:T(8,128)(2,1)}, u32[]{:S(2)}, u32[]{:S(2)}) collective-permute-start(bf16[4,96,2816]{2,1,0:T(8,128)(2,1)} %copy.171), channel_id=1, source_target_pairs={{0,4},{4,0},{8,12},{12,8},{16,20},{20,16},{24,28},{28,24},{1,5},{5... | collective-permute-start | bytes 6488072 | tf_op jit(solution)/shard_map/ppermute | solution.py:117
  425.3 256.9 %collective-permute-start.54 = (f32[256,768]{1,0:T(8,128)}, f32[256,768]{1,0:T(8,128)}, u32[]{:S(2)}, u32[]{:S(2)}) collective-permute-start(f32[256,768]{1,0:T(8,128)} %add.758), channel_id=1, source_target_pairs={{0,1},{1,0},{2,3},{3,2},{4,5},{5,4},{6,7},{7,6},{8,9},{9,8},{10,11... | collective-permute-start | bytes 2359304 | tf_op jit(solution)/shard_map/ppermute | solution.py:117
  425.6 253.5 %collective-permute-start.43 = (bf16[1,256,1024]{2,1,0:T(8,128)(2,1)}, bf16[1,256,1024]{2,1,0:T(8,128)(2,1)}, u32[]{:S(2)}, u32[]{:S(2)}) collective-permute-start(bf16[1,256,1024]{2,1,0:T(8,128)(2,1)} %slice.484), channel_id=1, source_target_pairs={{0,16},{4,20},{8,24},{12,28},{16,0},{20,4},{24,8},{28,12},{1,17},{... | collective-permute-start | bytes 1572872 | tf_op jit(solution)/shard_map/ppermute | solution.py:117
  647.7 56.5 %collective-permute-start.38 = (bf16[2,256,1024]{2,1,0:T(8,128)(2,1)}, bf16[2,256,1024]{2,1,0:T(8,128)(2,1)}, u32[]{:S(2)}, u32[]{:S(2)}) collective-permute-start(bf16[2,256,1024]{2,1,0:T(8,128)(2,1)} %bitcast.45), channel_id=1, source_target_pairs={{0,8},{4,12},{8,0},{12,4},{16,24},{20,28},{24,16},{28,20},{1,9},{5... | collective-permute-start | bytes 3145736 | tf_op jit(solution)/shard_map/ppermute | solution.py:117
  653.7 16.2 %collective-permute-start.32 = (f32[262,16]{0,1:T(8,128)S(1)}, f32[262,16]{0,1:T(8,128)S(1)}, u32[]{:S(2)}, u32[]{:S(2)}) collective-permute-start(f32[262,16]{0,1:T(8,128)S(1)} %add.722), channel_id=1, source_target_pairs={{0,16},{4,20},{8,24},{12,28},{16,0},{20,4},{24,8},{28,12},{1,17},{... | collective-permute-start | bytes 50312 | tf_op jit(solution)/shard_map/ppermute | solution.py:117
  654.9 21.3 %collective-permute-start.34 = (f32[452,128]{1,0:T(8,128)}, f32[452,128]{1,0:T(8,128)}, u32[]{:S(2)}, u32[]{:S(2)}) collective-permute-start(f32[452,128]{1,0:T(8,128)} %fusion.149), channel_id=1, source_target_pairs={{0,8},{4,12},{8,0},{12,4},{16,24},{20,28},{24,16},{28,20},{1,9},{5... | collective-permute-start | bytes 694280 | tf_op jit(solution)/shard_map/ppermute | solution.py:117
  669.8 39.5 %collective-permute-start.49 = (bf16[2,96,2816]{2,1,0:T(8,128)(2,1)}, bf16[2,96,2816]{2,1,0:T(8,128)(2,1)S(1)}, u32[]{:S(2)}, u32[]{:S(2)}) collective-permute-start(bf16[2,96,2816]{2,1,0:T(8,128)(2,1)} %copy.173), channel_id=1, source_target_pairs={{0,8},{4,12},{8,0},{12,4},{16,24},{20,28},{24,16},{28,20},{1,9},{5... | collective-permute-start | bytes 3244040 | tf_op jit(solution)/shard_map/ppermute | solution.py:117
  678.0 25.1 %collective-permute-start.35 = (f32[452,128]{1,0:T(8,128)}, f32[452,128]{1,0:T(8,128)}, u32[]{:S(2)}, u32[]{:S(2)}) collective-permute-start(f32[452,128]{1,0:T(8,128)} %fusion.257), channel_id=1, source_target_pairs={{0,16},{4,20},{8,24},{12,28},{16,0},{20,4},{24,8},{28,12},{1,17},{... | collective-permute-start | bytes 694280 | tf_op jit(solution)/shard_map/ppermute | solution.py:117
  706.6 36.9 %collective-permute-start.39 = (bf16[1,256,1024]{2,1,0:T(8,128)(2,1)}, bf16[1,256,1024]{2,1,0:T(8,128)(2,1)}, u32[]{:S(2)}, u32[]{:S(2)}) collective-permute-start(bf16[1,256,1024]{2,1,0:T(8,128)(2,1)} %slice.480), channel_id=1, source_target_pairs={{0,16},{4,20},{8,24},{12,28},{16,0},{20,4},{24,8},{28,12},{1,17},{... | collective-permute-start | bytes 1572872 | tf_op jit(solution)/shard_map/ppermute | solution.py:117
  714.2 40.8 %collective-permute-start.50 = (bf16[1,96,2816]{2,1,0:T(8,128)(2,1)}, bf16[1,96,2816]{2,1,0:T(8,128)(2,1)S(1)}, u32[]{:S(2)}, u32[]{:S(2)}) collective-permute-start(bf16[1,96,2816]{2,1,0:T(8,128)(2,1)} %copy.175), channel_id=1, source_target_pairs={{0,16},{4,20},{8,24},{12,28},{16,0},{20,4},{24,8},{28,12},{1,17},{... | collective-permute-start | bytes 1622024 | tf_op jit(solution)/shard_map/ppermute | solution.py:117
  (158 other events, 1280.4 us)
